TPU v7x, 32 devices: a whole 2x2x4 slice. The times are simulated.
32 devices in a mesh: grp: 2 (over y), sta: 4 (over z), hr: 2 (over x), sub: 2 (over core).
Axes of the slice: x: 2, y: 2, z: 4, core: 2. Of those that a mesh axis runs over, the one named last changes fastest.
Arguments:
- spectra: bfloat16 [4, 1000, 2, 4096], P(('grp', 'hr'), 'sub', None, 'sta'), parts along dimension 0, may hold values from -400 to 400
- pair_blocks: int32 [4, 2], replicated, may hold values from 0 to 31, as said below
- pair_owner: int32 [4], replicated, may hold values from 0 to 3, as said below
- block_members: int32 [32, 128], P('sta'), may hold values from 0 to 1023, as said below
Outputs:
- correlations: bfloat16 [32, 12, 128, 128], P(('grp', 'hr', 'sub'), 'sta'), parts along dimension 0
There are 2 independent parts, one for each index of `grp`. A program takes and returns all parts, laid end to end along the dimension named above; an argument that names none is the same for every part. Nothing has to cross between parts.
Inputs may be any that keep to these rules, and one draw needn't show every extreme that they name: `pair_blocks`: each row names two different blocks; block g holds stations of index g // 8 of sta. The blocks of the pairs of owner o lie on indices o, o + 1, o + 2 or o + 3 (mod 4) of sta, and the distinct blocks named by the pairs of one owner lie on distinct indices of sta. `pair_owner`: at most 3 pairs share an owner, and some owner has exactly 3. `block_members`: the 8 rows of the blocks of one index of sta hold each of 0 to 1023 once.
All inputs are finite; a program needn't handle non-finite values.
Results may differ from a plain program's by a relative error of at most 0.0063.
Values may be sent and summed in bfloat16 or wider, within the bound.
No kernel may reach another device: no remote copies, remote signals or barrier semaphores. Data moves between devices by JAX's collectives and lax.ppermute only.
A program may use at most 64 MiB of HBM per device.

v0:
```python
import functools
import itertools
import math

import jax
import jax.numpy as jnp
import numpy as np
from jax import lax
from jax.experimental import pallas as pl
from jax.experimental.pallas import tpu as pltpu
from jax.sharding import PartitionSpec as P

BAND = 50
LAGS = 16
CAP = 3
REACH = 4
COPIES = 2
EPSILON = 1e-05
LANES = 128
F32 = jnp.float32
BF16 = jnp.bfloat16
PICK_VMEM_LIMIT = 59 * 1024 * 1024
LAG_VMEM_LIMIT = 32 * 1024 * 1024

NT = (((1,), (1,)), ((), ()))


def dot_nt(left, right):
    return lax.dot_general(left, right, NT, preferred_element_type=F32)


def iota(shape, dim):
    return lax.broadcasted_iota(jnp.int32, shape, dim)


def send_keys(first, second, sta_count, where):
    keys = [0]
    for reach in range(2, REACH):
        first_sends = (first - second - reach) % sta_count == 0
        keys.append(where(first_sends, REACH, 0) + reach)
    return keys


def read_pairs(pair_ref, owner_ref, block_count):
    pairs = []
    for pair in range(owner_ref.shape[0]):
        blocks = [pair_ref[side, pair] for side in range(2)]
        pairs.append((owner_ref[pair], blocks, [lax.div(block, block_count) for block in blocks]))
    return pairs


def case_of(pairs, sta_count):
    first = second = needs = jnp.int32(0)
    for owner, _, homes in pairs:
        count = jnp.int32(0)
        for other, _, _ in pairs:
            count = count + (other == owner).astype(jnp.int32)
        ends = [lax.rem(home - owner + sta_count, sta_count) for home in homes]
        first = jnp.where(count == CAP, owner, first)
        second = jnp.where(count < CAP, owner, second)
        needs = jnp.where(count < CAP, (1 << ends[0]) | (1 << ends[1]), needs)
    return first, second, case_number(first, second, needs, sta_count)


def pick_kernel(kept, branched, sta_axis, pair_hbm, owner_hbm, member_hbm, case_hbm, x_ref, *rest):
    outs = rest[:REACH]
    pair_ref, owner_ref, member_ref, case_ref, number_ref, x_buf, y_buf, white_buf, sems = rest[
        REACH + branched :
    ]
    if branched:
        branch_copy = pltpu.make_async_copy(number_ref, rest[REACH], sems.at[COPIES + 4])
    freqs, tiles = x_buf.shape[0], x_buf.shape[2] // LANES
    block_count, width = member_ref.shape
    rows = y_buf.shape[0]
    chunks = rows // (2 * LANES)

    def fetch(part):
        run = pl.ds(part * (freqs // COPIES), freqs // COPIES)
        return pltpu.make_async_copy(x_ref.at[0, run], x_buf.at[run], sems.at[part])

    small = [
        pltpu.make_async_copy(source, target, sems.at[COPIES + index])
        for index, (source, target) in enumerate(
            (
                (pair_hbm, pair_ref),
                (owner_hbm, owner_ref),
                (member_hbm, member_ref),
                (case_hbm, case_ref),
            )
        )
    ]
    for copy in small:
        copy.start()
    for part in range(COPIES):
        fetch(part).start()

    def bands(shape, part_dim):
        part, place = iota(shape, part_dim), iota(shape, 1 - part_dim)
        low = (place % 16) * (2 * BAND)
        hit = (part >= low) & (part < low + 2 * BAND) & (part < 2 * freqs) & (place < 48)
        return jnp.where(hit, 1.0, 0.0).astype(BF16)

    gather_bands, spread_bands = bands((48, rows), 1), bands((rows, LANES), 0)
    row, col = iota((2 * LANES, 2 * LANES), 0), iota((2 * LANES, 2 * LANES), 1)
    split = jnp.where(row == 2 * (col % LANES) + col // LANES, 1.0, 0.0).astype(BF16)
    y_buf[2 * freqs :] = jnp.zeros((rows - 2 * freqs, kept * width), F32)
    for copy in small:
        copy.wait()

    my_sta = lax.axis_index(sta_axis)
    sta_count = lax.axis_size(sta_axis)
    pairs = read_pairs(pair_ref, owner_ref, block_count)
    found, wanted = jnp.int32(0), []
    for reach in range(REACH):
        owner = lax.rem(my_sta - reach + REACH * sta_count, sta_count)
        chosen = jnp.int32(-1)
        for pair_owner, blocks, homes in pairs:
            for block, home in zip(blocks, homes):
                hit = (pair_owner == owner) & (home == my_sta)
                chosen = jnp.where(hit, lax.rem(block, block_count), chosen)
        wanted.append((found, chosen))
        found = found + (chosen >= 0).astype(jnp.int32)
    places, station = [], []
    for place in range(kept):
        reach_here, block_here = jnp.int32(-1), jnp.int32(0)
        for reach, (rank, chosen) in enumerate(wanted):
            hit = (rank == place) & (chosen >= 0)
            reach_here = jnp.where(hit, reach, reach_here)
            block_here = jnp.where(hit, chosen, block_here)
        places.append(reach_here)
        station.append(member_ref[pl.ds(block_here, 1), :])
    station = jnp.concatenate(station, axis=1)
    hot = jnp.where(station == iota((tiles * LANES, kept * width), 0), 1.0, 0.0).astype(BF16)

    if branched:
        number_ref[0] = case_ref[case_of(pairs, sta_count)[2]]
        branch_copy.start()

    for part in range(COPIES):
        fetch(part).wait()
    x = jnp.concatenate(
        [
            x_buf[:, :, tile * LANES : (tile + 1) * LANES].reshape(2 * freqs, LANES)
            for tile in range(tiles)
        ],
        axis=1,
    )
    y_buf[: 2 * freqs] = jnp.dot(x, hot, preferred_element_type=F32)

    values = y_buf[...]
    square = values * values
    high = square.astype(BF16)
    low = (square - high.astype(F32)).astype(BF16)
    power = jnp.dot(gather_bands, high, preferred_element_type=F32)
    power += jnp.dot(gather_bands, low, preferred_element_type=F32)
    scale = lax.rsqrt(power * (1.0 / (2 * BAND)) + EPSILON)
    high = scale.astype(BF16).astype(F32)
    mid = (scale - high).astype(BF16).astype(F32)
    low = scale - high - mid
    third = iota(scale.shape, 0) // 16
    pieces = jnp.where(third == 0, high, jnp.where(third == 1, mid, low))
    pieces = jnp.concatenate(
        [pieces, jnp.zeros((LANES - pieces.shape[0], pieces.shape[1]), F32)], axis=0
    ).astype(BF16)
    white = y_buf[...] * jnp.dot(spread_bands, pieces, preferred_element_type=F32)
    white = white.astype(BF16)
    parted = []
    for chunk in range(chunks):
        mixed = white[chunk * 2 * LANES : (chunk + 1) * 2 * LANES]
        part = lax.dot_general(
            mixed, split, (((0,), (0,)), ((), ())), preferred_element_type=F32
        )
        parted.append(part.astype(BF16))
    white_buf[...] = jnp.concatenate(
        [part[:, :LANES] for part in parted] + [part[:, LANES:] for part in parted], axis=1
    )
    for place, reach_here in enumerate(places):
        for reach in range(REACH):

            @pl.when(reach_here == reach)
            def _():
                outs[reach][...] = white_buf[place * width : (place + 1) * width]

    if branched:
        branch_copy.wait()


def pick_blocks(kept, branched, spectra, pair_sides, pair_owner, block_members, case_table):
    _, freqs, parts, stations = spectra.shape
    block_count, width = block_members.shape
    columns = -(-freqs // LANES) * 2 * LANES
    rows = kept * width
    vmem = pl.BlockSpec(memory_space=pltpu.VMEM)
    out_shape = [jax.ShapeDtypeStruct((width, columns), BF16)] * REACH
    out_shape += [jax.ShapeDtypeStruct((1,), jnp.int32)] * branched
    return pl.pallas_call(
        functools.partial(pick_kernel, kept, branched, "sta"),
        out_shape=out_shape,
        in_specs=[pl.BlockSpec(memory_space=pltpu.HBM)] * 5,
        out_specs=[vmem] * REACH + [pl.BlockSpec(memory_space=pltpu.HBM)] * branched,
        scratch_shapes=[
            pltpu.SMEM(pair_sides.shape, jnp.int32),
            pltpu.SMEM(pair_owner.shape, jnp.int32),
            pltpu.VMEM(block_members.shape, jnp.int32),
            pltpu.SMEM(case_table.shape, jnp.int32),
            pltpu.SMEM((1,), jnp.int32),
            pltpu.VMEM((freqs, parts, stations), BF16),
            pltpu.VMEM((columns, rows), F32),
            pltpu.VMEM((rows, columns), BF16),
            pltpu.SemaphoreType.DMA((COPIES + 5,)),
        ],
        compiler_params=pltpu.CompilerParams(vmem_limit_bytes=PICK_VMEM_LIMIT),
        cost_estimate=pl.CostEstimate(
            flops=2 * rows * stations * freqs * parts,
            bytes_accessed=2 * spectra.size + 4 * rows * columns,
            transcendentals=0,
        ),
        name="pick_and_whiten",
    )(pair_sides, pair_owner, block_members, case_table, spectra)


def case_number(first, second, needs, sta_count):
    return (first * sta_count + second) * (1 << (REACH - 1)) + needs // 2


def routes(sta_count):
    def load(first, second, sent):
        links = {}
        flows = [((home + 1) % sta_count, home) for home in range(sta_count)]
        flows += [((first + reach) % sta_count, first) for reach in range(2, REACH)]
        flows += [((second + reach) % sta_count, second) for reach in sent]
        for source, owner in flows:
            step = 1 if owner > source else -1
            for place in range(source, owner, step):
                links[place, step] = links.get((place, step), 0) + 1
        return max(links.values())

    far = range(2, REACH)
    sets = [sent for count in range(len(far), -1, -1) for sent in itertools.combinations(far, count)]
    branches = []
    cases = [0] * case_number(sta_count, 0, 0, sta_count)
    for first, second in itertools.permutations(range(sta_count), 2):
        for named in itertools.combinations(range(REACH), 2):
            fits = [sent for sent in sets if set(named) - {0, 1} <= set(sent)]
            branch = (first, second, min(fits, key=lambda sent: load(first, second, sent)))
            if branch not in branches:
                branches.append(branch)
            needs = sum(1 << reach for reach in named)
            cases[case_number(first, second, needs, sta_count)] = branches.index(branch)
    return branches, cases


def phase_tables(sub_count, sub_freqs, groups, lag_rows):
    chunks = -(-sub_freqs // LANES)
    total = sub_count * sub_freqs
    freq = np.arange(total, dtype=np.int64).reshape(sub_count, 1, sub_freqs)
    middle = [2 * (group * lag_rows - LAGS // 2) + lag_rows - 1 for group in range(groups)]
    away = [step for step in range(1, lag_rows) if step % 2 != lag_rows % 2]

    def table(twice, forms, tile, dtype):
        twice = np.array(twice or [0], dtype=np.int64).reshape(1, -1, 1)
        angle = np.mod(freq * twice, 2 * total) * (math.pi / total)
        rows = np.stack([form(angle) for form in forms], axis=2)
        rows = rows.reshape(sub_count, -1, sub_freqs)
        pad = ((0, 0), (0, -rows.shape[1] % tile), (0, chunks * LANES - sub_freqs))
        return np.pad(rows, pad).astype(np.float32).astype(dtype)

    turns = table(middle, (np.cos, np.sin), 8, np.float32)
    offsets = table(away, (np.cos, np.sin, lambda angle: -np.sin(angle)), 16, BF16)
    return turns, offsets, len(away)


def lag_kernel(hops, slots, lag_rows, away, block_count, branched, *refs):
    sub_count = lax.axis_size("sub")
    hr_count = lax.axis_size("hr")
    pair_ref, owner_ref, turn_ref, offset_ref = refs[:4]
    blocks, outs = refs[4 : -2 - len(hops)], refs[-2 - len(hops) : -2]
    buf, sems = refs[-2:]
    width = buf.shape[3]
    span = buf.shape[4] // 2
    middle_lag = lag_rows % 2
    my_sub = lax.axis_index("sub")
    my_hr = lax.axis_index("hr")
    my_sta = lax.axis_index("sta")
    sta_count = lax.axis_size("sta")

    pairs = read_pairs(pair_ref, owner_ref, block_count)
    order = [jnp.int32(reach) for reach in range(REACH)]
    if branched:
        first, second, _ = case_of(pairs, sta_count)
        keys = send_keys(first, second, sta_count, jnp.where)
        for reach, key in enumerate(keys):
            order[1 + reach] = 1 + sum(jnp.int32(other < key) for other in keys)
    owned = []
    for owner, _, homes in pairs:
        places = []
        for home in homes:
            reach_here = lax.rem(home - my_sta + sta_count, sta_count)
            place_here = order[0]
            for reach in range(1, REACH):
                place_here = jnp.where(reach_here == reach, order[reach], place_here)
            places.append(place_here)
        owned.append((owner == my_sta, places))
    ends = []
    for slot in slots:
        count = jnp.int32(0)
        slot_ends = [jnp.int32(-1)] * 2
        for mine, places in owned:
            hit = mine & (count == slot)
            count = count + mine.astype(jnp.int32)
            slot_ends = [jnp.where(hit, new, old) for new, old in zip(places, slot_ends)]
        ends.append(slot_ends)

    def fetches(index, act):
        for side in range(2):
            for place in range(REACH):

                @pl.when(ends[index][side] == place)
                def _():
                    for step in range(sub_count):
                        act(
                            pltpu.make_async_copy(
                                blocks[place * sub_count + step],
                                buf.at[index, side, step],
                                sems.at[index, side, step],
                            )
                        )

    for index in range(len(slots)):
        fetches(index, lambda copy: copy.start())

    for index in range(len(slots)):

        @pl.when(ends[index][0] < 0)
        def _():
            for out in outs:
                out[:, index] = jnp.zeros((lag_rows, width, width), out.dtype)

        fetches(index, lambda copy: copy.wait())

        @pl.when(ends[index][0] >= 0)
        def _():
            total = None
            for step in range(sub_count):
                sub = lax.rem(my_sub + step, sub_count)
                real = buf[index, 0, step, :, :span]
                imag = buf[index, 0, step, :, span:]
                scaled_real, scaled_imag = [real] * middle_lag, [imag] * middle_lag
                for near in range(away):
                    cosine, sine, minus = (
                        offset_ref[sub, 3 * near + form : 3 * near + form + 1, :]
                        for form in range(3)
                    )
                    scaled_real += [real * cosine, imag * minus]
                    scaled_imag += [imag * cosine, real * sine]
                real = buf[index, 1, step, :, :span].astype(F32)
                imag = buf[index, 1, step, :, span:].astype(F32)
                turned_real, turned_imag = [], []
                for hop in hops:
                    group = lax.rem(my_hr + hop, hr_count) * sub_count + my_sub
                    cosine = turn_ref[sub, pl.ds(2 * group, 1), :]
                    sine = turn_ref[sub, pl.ds(2 * group + 1, 1), :]
                    turned_real.append((real * cosine + imag * sine).astype(BF16))
                    turned_imag.append((imag * cosine - real * sine).astype(BF16))
                for scaled, turned in ((scaled_real, turned_real), (scaled_imag, turned_imag)):
                    part = dot_nt(jnp.concatenate(scaled, axis=0), jnp.concatenate(turned, axis=0))
                    total = part if total is None else total + part
            for place, out in enumerate(outs):
                columns = slice(place * width, (place + 1) * width)
                if middle_lag:
                    out[lag_rows // 2, index] = total[:width, columns].astype(out.dtype)
                for near in range(away):
                    start = (middle_lag + 2 * near) * width
                    even = total[start : start + width, columns]
                    odd = total[start + width : start + 2 * width, columns]
                    below = (lag_rows - 1) // 2 - near - middle_lag
                    above = lag_rows - 1 - below
                    out[above, index] = (even + odd).astype(out.dtype)
                    out[below, index] = (even - odd).astype(out.dtype)


def on_device(spectra, pair_blocks, pair_owner, block_members):
    hour_count, sub_freqs, _, _ = spectra.shape
    block_count, width = block_members.shape
    sta_count, hr_count, sub_count = (lax.axis_size(axis) for axis in ("sta", "hr", "sub"))
    groups = hr_count * sub_count
    lag_rows = LAGS // groups
    norming = 1.0 / math.sqrt(hour_count * hr_count * sub_count * sub_freqs)
    pair_sides = pair_blocks.T
    turns, offsets, away = phase_tables(sub_count, sub_freqs, groups, lag_rows)

    owners_at_most = pair_owner.shape[0] - CAP + 1
    branched = owners_at_most == 2 and sta_count == REACH
    kept = min(REACH, owners_at_most)
    branches, cases = routes(sta_count) if branched else ([], [])
    case_table = jnp.asarray(np.array(cases or [0], dtype=np.int32))
    picked = pick_blocks(
        kept, branched, spectra, pair_sides, pair_owner, block_members, case_table
    )

    def exchange(owners_of, order, *picked):
        arrived = [picked[0]]
        for reach in order:
            to_owner = [((owner + reach) % sta_count, owner) for owner in owners_of[reach - 1]]
            arrived.append(lax.ppermute(picked[reach], "sta", to_owner))
        blocks = []
        for block in arrived:
            blocks.append(block)
            for step in range(1, sub_count):
                swap = [((sub + step) % sub_count, sub) for sub in range(sub_count)]
                blocks.append(lax.ppermute(block, "sub", swap))
        return blocks

    if branched:
        steps = []
        for first, second, sent in branches:
            owners_of = [range(sta_count)] + [
                (first, second) if reach in sent else (first,) for reach in range(2, REACH)
            ]
            keys = send_keys(first, second, sta_count, lambda hit, yes, no: yes if hit else no)
            order = sorted(range(1, REACH), key=lambda reach: keys[reach - 1])
            steps.append(functools.partial(exchange, owners_of, order))
        blocks = lax.switch(picked[REACH][0], steps, *picked[:REACH])
    else:
        blocks = exchange([range(sta_count)] * (REACH - 1), range(1, REACH), *picked[:REACH])

    smem = pl.BlockSpec(memory_space=pltpu.SMEM)
    vmem = pl.BlockSpec(memory_space=pltpu.VMEM)
    hbm = pl.BlockSpec(memory_space=pltpu.HBM)
    row = picked[0].shape[1]
    versions = (lag_rows % 2 + 2 * away) * width

    def products(hops, slots, dtype, name):
        return pl.pallas_call(
            functools.partial(
                lag_kernel, hops, slots, lag_rows, away, block_count, branched
            ),
            out_shape=[jax.ShapeDtypeStruct((lag_rows, len(slots), width, width), dtype)]
            * len(hops),
            in_specs=[smem, smem, vmem, vmem] + [hbm] * len(blocks),
            out_specs=[vmem] * len(hops),
            scratch_shapes=[
                pltpu.VMEM((len(slots), 2, sub_count, width, row), BF16),
                pltpu.SemaphoreType.DMA((len(slots), 2, sub_count)),
            ],
            compiler_params=pltpu.CompilerParams(vmem_limit_bytes=LAG_VMEM_LIMIT),
            cost_estimate=pl.CostEstimate(
                flops=2 * len(slots) * len(hops) * versions * width * sub_count * row,
                bytes_accessed=4 * len(slots) * sub_count * width * row,
                transcendentals=0,
            ),
            name=name,
        )(pair_sides, pair_owner, turns, offsets, *blocks)

    hops, slots = tuple(range(1, hr_count)), tuple(range(CAP))
    sent = products(hops, slots, BF16, "lags_to_send")
    received = []
    for hop, part in zip(hops, sent):
        to_device = [(hr, (hr + hop) % hr_count) for hr in range(hr_count)]
        received.append(lax.ppermute(part, "hr", to_device))
    (summed,) = products((0,), slots, F32, "lags_to_keep")
    for part in received:
        summed = summed + part.astype(F32)
    return (summed * norming).astype(BF16)


def solution(mesh):
    placed = (P(("grp", "hr"), "sub", None, "sta"), P(), P(), P("sta", None))
    return jax.shard_map(
        on_device,
        mesh=mesh,
        in_specs=placed,
        out_specs=P(("grp", "hr", "sub"), "sta", None, None),
        check_vma=False,
    )
```

profile of v0, /device:TPU:0, one launch (start us, length us, event | category | flops | bytes accessed | tf_op | source)
XLA Modules:
  0.0 45.0 jit_solution(18358625955492879810)
XLA Ops:
  0.0 3.8 %pick_and_whiten.1 = (bf16[128,1024]{1,0:T(8,128)(2,1)S(1)}, bf16[128,1024]{1,0:T(8,128)(2,1)S(1)}, bf16[128,1024]{1,0:T(8,128)(2,1)S(1)}, bf16[128,1024]{1,0:T(8,128)(2,1)S(1)}, s32[1]{0:T(128)}) custom-call(s32[2,4]{1,0:T(2,128)} %bitcast.2, s32[4]{0:T(128)} %refs_1_.3, s32[8,128]{1,0:T(8,128)} %member_hbm.1, s32[128]{0:T(128)} %constant.14.clone.case_hbm, ...), custom_call_target="tpu_custom_call" | custom-call | flops 524288000 | bytes 3096576 | tf_op jit(solution)/shard_map/pick_and_whiten/pallas_call | solution.py:196
  4.5 24.2 %conditional.1 = (bf16[128,1024]{1,0:T(8,128)(2,1)}, bf16[128,1024]{1,0:T(8,128)(2,1)}, bf16[128,1024]{1,0:T(8,128)(2,1)}, bf16[128,1024]{1,0:T(8,128)(2,1)}, bf...) conditional(s32[]{:T(128)} %bitcast.1, ...), branch_computations={%region_0.0_spmd, %region_1.0_spmd, %region_2.0_spmd, %region_3.0_... | conditional | bytes 7340368 | solution.py:423
  4.5 5.1 %collective-permute-start.22 = (bf16[128,1024]{1,0:T(8,128)(2,1)S(1)}, bf16[128,1024]{1,0:T(8,128)(2,1)}, u32[]{:S(2)}, u32[]{:S(2)}) collective-permute-start(bf16[128,1024]{1,0:T(8,128)(2,1)S(1)} %get-tuple-element.194), channel_id=1, source_target_pairs={{4,0},{8,4},{12,8},{0,12},{5,1},{9,5},{13,9},{1,13},{6,2},{10,6},{... | collective-permute-start | bytes 786440 | tf_op jit(solution)/shard_map/cond/branch_3_fun/ppermute | solution.py:405
  9.6 1.3 %collective-permute-start.24 = (bf16[128,1024]{1,0:T(8,128)(2,1)S(1)}, bf16[128,1024]{1,0:T(8,128)(2,1)}, u32[]{:S(2)}, u32[]{:S(2)}) collective-permute-start(bf16[128,1024]{1,0:T(8,128)(2,1)S(1)} %get-tuple-element.195), channel_id=1, source_target_pairs={{8,0},{4,12},{9,1},{5,13},{10,2},{6,14},{11,3},{7,15},{24,16},{20,... | collective-permute-start | bytes 786440 | tf_op jit(solution)/shard_map/cond/branch_3_fun/ppermute | solution.py:405
  10.9 1.3 %collective-permute-start.26 = (bf16[128,1024]{1,0:T(8,128)(2,1)S(1)}, bf16[128,1024]{1,0:T(8,128)(2,1)}, u32[]{:S(2)}, u32[]{:S(2)}) collective-permute-start(bf16[128,1024]{1,0:T(8,128)(2,1)S(1)} %get-tuple-element.196), channel_id=1, source_target_pairs={{12,0},{8,12},{13,1},{9,13},{14,2},{10,14},{15,3},{11,15},{28,16},... | collective-permute-start | bytes 786440 | tf_op jit(solution)/shard_map/cond/branch_3_fun/ppermute | solution.py:405
  12.2 0.1 collective-permute-start.21
  12.3 2.9 %collective-permute-done.22 = bf16[128,1024]{1,0:T(8,128)(2,1)} collective-permute-done((bf16[128,1024]{1,0:T(8,128)(2,1)S(1)}, bf16[128,1024]{1,0:T(8,128)(2,1)}, u32[]{:S(2)}, u32[]{:S(2)}) %collective-permute-start.22) | collective-permute-done | bytes 262176 | tf_op jit(solution)/shard_map/cond/branch_3_fun/ppermute | solution.py:405
  15.3 0.0 collective-permute-start.23
  15.3 11.2 %collective-permute-done.24 = bf16[128,1024]{1,0:T(8,128)(2,1)} collective-permute-done((bf16[128,1024]{1,0:T(8,128)(2,1)S(1)}, bf16[128,1024]{1,0:T(8,128)(2,1)}, u32[]{:S(2)}, u32[]{:S(2)}) %collective-permute-start.24) | collective-permute-done | bytes 262176 | tf_op jit(solution)/shard_map/cond/branch_3_fun/ppermute | solution.py:405
  26.5 0.0 collective-permute-start.25
  26.5 0.0 collective-permute-done.26
  26.5 0.5 %collective-permute-start.27 = (bf16[128,1024]{1,0:T(8,128)(2,1)}, bf16[128,1024]{1,0:T(8,128)(2,1)}, u32[]{:S(2)}, u32[]{:S(2)}) collective-permute-start(bf16[128,1024]{1,0:T(8,128)(2,1)} %collective-permute-done.26), channel_id=1, source_target_pairs={{1,0},{0,1},{3,2},{2,3},{5,4},{4,5},{7,6},{6,7},{9,8},{8,9},{11,10... | collective-permute-start | bytes 786440 | tf_op jit(solution)/shard_map/cond/branch_3_fun/ppermute | solution.py:411
  27.0 0.0 collective-permute-done.21
  27.0 0.0 collective-permute-done.23
  27.0 1.4 %collective-permute-done.25 = bf16[128,1024]{1,0:T(8,128)(2,1)} collective-permute-done((bf16[128,1024]{1,0:T(8,128)(2,1)}, bf16[128,1024]{1,0:T(8,128)(2,1)}, u32[]{:S(2)}, u32[]{:S(2)}) %collective-permute-start.25) | collective-permute-done | bytes 262176 | tf_op jit(solution)/shard_map/cond/branch_3_fun/ppermute | solution.py:411
  28.3 0.4 collective-permute-done.27
  28.7 0.0 copy-done.2
  28.7 0.0 copy-done.3
  28.7 0.0 copy-done.1
  28.7 4.2 %lags_to_send.1 = bf16[4,3,128,128]{3,2,1,0:T(8,128)(2,1)S(1)} custom-call(s32[2,4]{1,0:T(2,128)S(1)} %bitcast.3, s32[4]{0:T(128)S(1)} %copy-done.1, f32[2,8,512]{2,1,0:T(8,128)S(1)} %copy-done.3, bf16[2,16,512]{2,1,0:T(8,128)(2,1)S(1)} %copy-done.2, bf16[128,1024]{1,0:T(8,128)(2,1)S(1)} %get-tuple-element.281.refs_4_, ...), custom_call_target="tpu_custom_call" | custom-call | flops 805306368 | bytes 3145728 | tf_op jit(solution)/shard_map/lags_to_send/pallas_call | solution.py:434
  32.9 1.6 %collective-permute-start.154 = (bf16[4,3,128,128]{3,2,1,0:T(8,128)(2,1)S(1)}, bf16[4,3,128,128]{3,2,1,0:T(8,128)(2,1)S(1)}, u32[]{:S(2)}, u32[]{:S(2)}) collective-permute-start(bf16[4,3,128,128]{3,2,1,0:T(8,128)(2,1)S(1)} %lags_to_send.1), channel_id=1, source_target_pairs={{0,2},{2,0},{1,3},{3,1},{4,6},{6,4},{5,7},{7,5},{8,10},{10,8},{9,1... | collective-permute-start | bytes 1179656 | tf_op jit(solution)/shard_map/ppermute | solution.py:460
  34.5 4.2 %lags_to_keep.1 = f32[4,3,128,128]{3,2,1,0:T(8,128)S(1)} custom-call(s32[2,4]{1,0:T(2,128)S(1)} %bitcast.4, s32[4]{0:T(128)S(1)} %copy-done.1, f32[2,8,512]{2,1,0:T(8,128)S(1)} %copy-done.3, bf16[2,16,512]{2,1,0:T(8,128)(2,1)S(1)} %copy-done.2, bf16[128,1024]{1,0:T(8,128)(2,1)S(1)} %get-tuple-element.281.refs_4_, ...), custom_call_target="tpu_custom_call" | custom-call | flops 805306368 | bytes 3145728 | tf_op jit(solution)/shard_map/lags_to_keep/pallas_call | solution.py:434
  38.6 5.5 %collective-permute-done.154 = bf16[4,3,128,128]{3,2,1,0:T(8,128)(2,1)S(1)} collective-permute-done((bf16[4,3,128,128]{3,2,1,0:T(8,128)(2,1)S(1)}, bf16[4,3,128,128]{3,2,1,0:T(8,128)(2,1)S(1)}, u32[]{:S(2)}, u32[]{:S(2)}) %collective-permute-start.154) | collective-permute-done | bytes 393248 | tf_op jit(solution)/shard_map/ppermute | solution.py:460
  44.1 0.9 %multiply_convert_fusion = bf16[4,3,128,128]{3,2,1,0:T(8,128)(2,1)} fusion(f32[4,3,128,128]{3,2,1,0:T(8,128)S(1)} %lags_to_keep.1, bf16[4,3,128,128]{3,2,1,0:T(8,128)(2,1)S(1)} %collective-permute-done.154), kind=kLoop, calls=%fused_computation | loop fusion | flops 786432 | bytes 1572864 | tf_op jit(solution)/shard_map/convert_element_type | solution.py:464
  (5 shorter events, 0.0 us)
Async XLA Ops:
  0.0 28.7 %copy-start.2 = (bf16[2,16,512]{2,1,0:T(8,128)(2,1)S(1)}, bf16[2,16,512]{2,1,0:T(8,128)(2,1)}, u32[]{:S(2)}) copy-start(bf16[2,16,512]{2,1,0:T(8,128)(2,1)} %constant.16.clone.refs_3_) | copy-start | bytes 98308
  0.0 28.7 %copy-start.3 = (f32[2,8,512]{2,1,0:T(8,128)S(1)}, f32[2,8,512]{2,1,0:T(8,128)}, u32[]{:S(2)}) copy-start(f32[2,8,512]{2,1,0:T(8,128)} %constant.15.clone.refs_2_) | copy-start | bytes 98308
  0.0 28.7 %copy-start.1 = (s32[4]{0:T(128)S(1)}, s32[4]{0:T(128)}, u32[]{:S(2)}) copy-start(s32[4]{0:T(128)} %refs_1_.3) | copy-start | bytes 52
  0.0 28.7 %copy-start = (s32[4,2]{0,1:T(2,128)S(1)}, s32[4,2]{0,1:T(2,128)}, u32[]{:S(2)}) copy-start(s32[4,2]{0,1:T(2,128)} %param.30) | copy-start | bytes 100
  4.5 10.8 %collective-permute-start.22 = (bf16[128,1024]{1,0:T(8,128)(2,1)S(1)}, bf16[128,1024]{1,0:T(8,128)(2,1)}, u32[]{:S(2)}, u32[]{:S(2)}) collective-permute-start(bf16[128,1024]{1,0:T(8,128)(2,1)S(1)} %get-tuple-element.194), channel_id=1, source_target_pairs={{4,0},{8,4},{12,8},{0,12},{5,1},{9,5},{13,9},{1,13},{6,2},{10,6},{... | collective-permute-start | bytes 786440 | tf_op jit(solution)/shard_map/cond/branch_3_fun/ppermute | solution.py:405
  9.6 16.8 %collective-permute-start.24 = (bf16[128,1024]{1,0:T(8,128)(2,1)S(1)}, bf16[128,1024]{1,0:T(8,128)(2,1)}, u32[]{:S(2)}, u32[]{:S(2)}) collective-permute-start(bf16[128,1024]{1,0:T(8,128)(2,1)S(1)} %get-tuple-element.195), channel_id=1, source_target_pairs={{8,0},{4,12},{9,1},{5,13},{10,2},{6,14},{11,3},{7,15},{24,16},{20,... | collective-permute-start | bytes 786440 | tf_op jit(solution)/shard_map/cond/branch_3_fun/ppermute | solution.py:405
  10.9 15.5 %collective-permute-start.26 = (bf16[128,1024]{1,0:T(8,128)(2,1)S(1)}, bf16[128,1024]{1,0:T(8,128)(2,1)}, u32[]{:S(2)}, u32[]{:S(2)}) collective-permute-start(bf16[128,1024]{1,0:T(8,128)(2,1)S(1)} %get-tuple-element.196), channel_id=1, source_target_pairs={{12,0},{8,12},{13,1},{9,13},{14,2},{10,14},{15,3},{11,15},{28,16},... | collective-permute-start | bytes 786440 | tf_op jit(solution)/shard_map/cond/branch_3_fun/ppermute | solution.py:405
  12.2 14.7 %collective-permute-start.21 = (bf16[128,1024]{1,0:T(8,128)(2,1)S(1)}, bf16[128,1024]{1,0:T(8,128)(2,1)}, u32[]{:S(2)}, u32[]{:S(2)}) collective-permute-start(bf16[128,1024]{1,0:T(8,128)(2,1)S(1)} %get-tuple-element.193), channel_id=1, source_target_pairs={{1,0},{0,1},{3,2},{2,3},{5,4},{4,5},{7,6},{6,7},{9,8},{8,9},{11,10... | collective-permute-start | bytes 786440 | tf_op jit(solution)/shard_map/cond/branch_3_fun/ppermute | solution.py:411
  15.3 11.7 %collective-permute-start.23 = (bf16[128,1024]{1,0:T(8,128)(2,1)}, bf16[128,1024]{1,0:T(8,128)(2,1)}, u32[]{:S(2)}, u32[]{:S(2)}) collective-permute-start(bf16[128,1024]{1,0:T(8,128)(2,1)} %collective-permute-done.22), channel_id=1, source_target_pairs={{1,0},{0,1},{3,2},{2,3},{5,4},{4,5},{7,6},{6,7},{9,8},{8,9},{11,10... | collective-permute-start | bytes 786440 | tf_op jit(solution)/shard_map/cond/branch_3_fun/ppermute | solution.py:411
  26.5 1.9 %collective-permute-start.25 = (bf16[128,1024]{1,0:T(8,128)(2,1)}, bf16[128,1024]{1,0:T(8,128)(2,1)}, u32[]{:S(2)}, u32[]{:S(2)}) collective-permute-start(bf16[128,1024]{1,0:T(8,128)(2,1)} %collective-permute-done.24), channel_id=1, source_target_pairs={{1,0},{0,1},{3,2},{2,3},{5,4},{4,5},{7,6},{6,7},{9,8},{8,9},{11,10... | collective-permute-start | bytes 786440 | tf_op jit(solution)/shard_map/cond/branch_3_fun/ppermute | solution.py:411
  26.5 2.2 %collective-permute-start.27 = (bf16[128,1024]{1,0:T(8,128)(2,1)}, bf16[128,1024]{1,0:T(8,128)(2,1)}, u32[]{:S(2)}, u32[]{:S(2)}) collective-permute-start(bf16[128,1024]{1,0:T(8,128)(2,1)} %collective-permute-done.26), channel_id=1, source_target_pairs={{1,0},{0,1},{3,2},{2,3},{5,4},{4,5},{7,6},{6,7},{9,8},{8,9},{11,10... | collective-permute-start | bytes 786440 | tf_op jit(solution)/shard_map/cond/branch_3_fun/ppermute | solution.py:411
  32.9 11.2 %collective-permute-start.154 = (bf16[4,3,128,128]{3,2,1,0:T(8,128)(2,1)S(1)}, bf16[4,3,128,128]{3,2,1,0:T(8,128)(2,1)S(1)}, u32[]{:S(2)}, u32[]{:S(2)}) collective-permute-start(bf16[4,3,128,128]{3,2,1,0:T(8,128)(2,1)S(1)} %lags_to_send.1), channel_id=1, source_target_pairs={{0,2},{2,0},{1,3},{3,1},{4,6},{6,4},{5,7},{7,5},{8,10},{10,8},{9,1... | collective-permute-start | bytes 1179656 | tf_op jit(solution)/shard_map/ppermute | solution.py:460
where the time goes:
time: 45.3 us; the launch traced here: 45 us
  waiting for transfers between devices  21.4 us (47%)
  Pallas kernels  12.1 us (27%)
  starting transfers between devices  9.86 us (22%)
  other arithmetic  0.87 us (2%)
  between operations  0.69 us (2%)
    ppermute x3, waiting for transfers between devices, exchange(): arrived.append(lax.ppermute(picked[reach], 'sta', to_owner))  14.1 us
    pallas_call x2, Pallas kernels, products(): pl.pallas_call(functools.partial(lag_kernel, hops, slots, lag_rows, away,...  8.34 us
    ppermute x3, starting transfers between devices, exchange(): arrived.append(lax.ppermute(picked[reach], 'sta', to_owner))  7.72 us
    ppermute x1, waiting for transfers between devices, on_device(): received.append(lax.ppermute(part, 'hr', to_device))  5.5 us
    pallas_call x1, Pallas kernels, pick_blocks(): pl.pallas_call(functools.partial(pick_kernel, kept, branched, 'sta'), out...  3.8 us
    ppermute x4, waiting for transfers between devices, exchange(): blocks.append(lax.ppermute(block, 'sub', swap))  1.74 us
    ppermute x1, starting transfers between devices, on_device(): received.append(lax.ppermute(part, 'hr', to_device))  1.55 us
  transfers between devices with their start and end apart: 8, of which 5 were waited for; matrix products, arithmetic and copies ran while one was open for 0% of the time, Pallas kernels for 9%

commit v1 on v0

--- a/solution.py
+++ b/solution.py
@@ -34,10 +34,11 @@
 
 
 def send_keys(first, second, sta_count, where):
-    keys = [0]
-    for reach in range(2, REACH):
-        first_sends = (first - second - reach) % sta_count == 0
-        keys.append(where(first_sends, REACH, 0) + reach)
+    keys = []
+    for reach in range(1, REACH):
+        distance = abs((first + reach) % sta_count - first)
+        alone = (first - second - reach) % sta_count == 0
+        keys.append((2 * distance + where(alone, 0, 1)) * REACH + reach)
     return keys
 
 
@@ -226,8 +227,7 @@
 def routes(sta_count):
     def load(first, second, sent):
         links = {}
-        flows = [((home + 1) % sta_count, home) for home in range(sta_count)]
-        flows += [((first + reach) % sta_count, first) for reach in range(2, REACH)]
+        flows = [((first + reach) % sta_count, first) for reach in range(1, REACH)]
         flows += [((second + reach) % sta_count, second) for reach in sent]
         for source, owner in flows:
             step = 1 if owner > source else -1
@@ -235,13 +235,15 @@
                 links[place, step] = links.get((place, step), 0) + 1
         return max(links.values())
 
-    far = range(2, REACH)
-    sets = [sent for count in range(len(far), -1, -1) for sent in itertools.combinations(far, count)]
+    every = range(1, REACH)
+    sets = [every, *itertools.combinations(every, len(every) - 1)]
     branches = []
     cases = [0] * case_number(sta_count, 0, 0, sta_count)
     for first, second in itertools.permutations(range(sta_count), 2):
+        own = (first - second) % sta_count
         for named in itertools.combinations(range(REACH), 2):
-            fits = [sent for sent in sets if set(named) - {0, 1} <= set(sent)]
+            fits = [sent for sent in sets if set(named) - {0} <= set(sent)]
+            fits = [sent for sent in fits if own in named or own not in sent] or fits
             branch = (first, second, min(fits, key=lambda sent: load(first, second, sent)))
             if branch not in branches:
                 branches.append(branch)
@@ -398,31 +400,46 @@
         kept, branched, spectra, pair_sides, pair_owner, block_members, case_table
     )
 
-    def exchange(owners_of, order, *picked):
-        arrived = [picked[0]]
+    def halves(block):
+        blocks = [block]
+        for step in range(1, sub_count):
+            swap = [((sub + step) % sub_count, sub) for sub in range(sub_count)]
+            blocks.append(lax.ppermute(block, "sub", swap))
+        return blocks
+
+    def to_owners(block, reach, owners):
+        pairs = [((owner + reach) % sta_count, owner) for owner in owners]
+        return lax.ppermute(block, "sta", pairs)
+
+    def exchange(*picked):
+        blocks = []
+        for reach in range(1, REACH):
+            blocks += halves(to_owners(picked[reach], reach, range(sta_count)))
+        return halves(picked[0]) + blocks
+
+    def exchange_two(first, second, sent, *picked):
+        own = (first - second) % sta_count
+        keys = send_keys(first, second, sta_count, lambda hit, yes, no: yes if hit else no)
+        order = sorted(range(1, REACH), key=lambda reach: keys[reach - 1])
+        arrived = {}
         for reach in order:
-            to_owner = [((owner + reach) % sta_count, owner) for owner in owners_of[reach - 1]]
-            arrived.append(lax.ppermute(picked[reach], "sta", to_owner))
-        blocks = []
-        for block in arrived:
-            blocks.append(block)
-            for step in range(1, sub_count):
-                swap = [((sub + step) % sub_count, sub) for sub in range(sub_count)]
-                blocks.append(lax.ppermute(block, "sub", swap))
+            owners = (first, second) if reach in sent and reach != own else (first,)
+            arrived[reach] = to_owners(picked[reach], reach, owners)
+        if own in sent:
+            block, _ = lax.optimization_barrier((picked[own], arrived[order[0]]))
+            block = to_owners(block, own, (second,))
+            here = lax.axis_index("sta") == second
+            arrived[own] = jnp.where(here, block, arrived[own])
+        blocks = halves(picked[0])
+        for reach in order:
+            blocks += halves(arrived[reach])
         return blocks
 
     if branched:
-        steps = []
-        for first, second, sent in branches:
-            owners_of = [range(sta_count)] + [
-                (first, second) if reach in sent else (first,) for reach in range(2, REACH)
-            ]
-            keys = send_keys(first, second, sta_count, lambda hit, yes, no: yes if hit else no)
-            order = sorted(range(1, REACH), key=lambda reach: keys[reach - 1])
-            steps.append(functools.partial(exchange, owners_of, order))
+        steps = [functools.partial(exchange_two, *branch) for branch in branches]
         blocks = lax.switch(picked[REACH][0], steps, *picked[:REACH])
     else:
-        blocks = exchange([range(sta_count)] * (REACH - 1), range(1, REACH), *picked[:REACH])
+        blocks = exchange(*picked[:REACH])
 
     smem = pl.BlockSpec(memory_space=pltpu.SMEM)
     vmem = pl.BlockSpec(memory_space=pltpu.VMEM)

time: 45.3 us -> 47.6 us (1.051)
  the two profiles are of different devices: /device:TPU:0 before, /device:TPU:24 now
where the time goes in v1:
time: 47.6 us; the launch traced here: 48.5 us
  waiting for transfers between devices  30 us (63%)
  Pallas kernels  9.51 us (20%)
  starting transfers between devices  7.05 us (15%)
  other arithmetic  0.87 us (2%)
  between operations  0.72 us (2%)
    ppermute x3, waiting for transfers between devices, to_owners(): return lax.ppermute(block, 'sta', pairs)  21.2 us
    ppermute x1, waiting for transfers between devices, on_device(): received.append(lax.ppermute(part, 'hr', to_device))  6.91 us
    pallas_call x2, Pallas kernels, products(): pl.pallas_call(functools.partial(lag_kernel, hops, slots, lag_rows, away,...  5.71 us
    ppermute x3, starting transfers between devices, to_owners(): return lax.ppermute(block, 'sta', pairs)  4.93 us
    pallas_call x1, Pallas kernels, pick_blocks(): pl.pallas_call(functools.partial(pick_kernel, kept, branched, 'sta'), out...  3.8 us
    ppermute x4, waiting for transfers between devices, halves(): blocks.append(lax.ppermute(block, 'sub', swap))  1.86 us
    ppermute x1, starting transfers between devices, on_device(): received.append(lax.ppermute(part, 'hr', to_device))  1.55 us
  transfers between devices with their start and end apart: 8, of which 4 were waited for; matrix products, arithmetic and copies ran while one was open for 0% of the time, Pallas kernels for 6%

profile of v1, /device:TPU:24, one launch (start us, length us, event | category | flops | bytes accessed | tf_op | source)
XLA Modules:
  0.0 48.5 jit_solution(6631695207791403856)
XLA Ops:
  0.0 3.8 %pick_and_whiten.1 = (bf16[128,1024]{1,0:T(8,128)(2,1)S(1)}, bf16[128,1024]{1,0:T(8,128)(2,1)S(1)}, bf16[128,1024]{1,0:T(8,128)(2,1)S(1)}, bf16[128,1024]{1,0:T(8,128)(2,1)S(1)}, s32[1]{0:T(128)}) custom-call(s32[2,4]{1,0:T(2,128)} %bitcast.2, s32[4]{0:T(128)} %refs_1_.3, s32[8,128]{1,0:T(8,128)} %member_hbm.1, s32[128]{0:T(128)} %constant.140.clone.case_hbm, ...), custom_call_target="tpu_custom_call" | custom-call | flops 524288000 | bytes 3096576 | tf_op jit(solution)/shard_map/pick_and_whiten/pallas_call | solution.py:197
  4.5 0.0 copy-start
  4.5 0.0 copy-start.1
  4.5 0.0 copy-start.2
  4.5 0.0 copy-start.3
  4.5 28.9 %conditional.1 = (bf16[128,1024]{1,0:T(8,128)(2,1)}, bf16[128,1024]{1,0:T(8,128)(2,1)}, bf16[128,1024]{1,0:T(8,128)(2,1)}, bf16[128,1024]{1,0:T(8,128)(2,1)}, bf...) conditional(s32[]{:T(128)} %bitcast.1, ...), branch_computations={%region_0.0_spmd, %region_1.2_spmd, %region_2.3_spmd, %region_3.4_... | conditional | flops 131076 | bytes 9175458 | solution.py:440
  4.7 1.4 %collective-permute-start.57 = (bf16[128,1024]{1,0:T(8,128)(2,1)S(1)}, bf16[128,1024]{1,0:T(8,128)(2,1)}, u32[]{:S(2)}, u32[]{:S(2)}) collective-permute-start(bf16[128,1024]{1,0:T(8,128)(2,1)S(1)} %get-tuple-element.338), channel_id=1, source_target_pairs={{4,8},{5,9},{6,10},{7,11},{20,24},{21,25},{22,26},{23,27}} | collective-permute-start | bytes 786440 | tf_op jit(solution)/shard_map/cond/branch_20_fun/ppermute | solution.py:412
  6.1 2.3 %collective-permute-start.59 = (bf16[128,1024]{1,0:T(8,128)(2,1)S(1)}, bf16[128,1024]{1,0:T(8,128)(2,1)}, u32[]{:S(2)}, u32[]{:S(2)}) collective-permute-start(bf16[128,1024]{1,0:T(8,128)(2,1)S(1)} %get-tuple-element.339), channel_id=1, source_target_pairs={{12,8},{0,12},{13,9},{1,13},{14,10},{2,14},{15,11},{3,15},{28,24},... | collective-permute-start | bytes 786440 | tf_op jit(solution)/shard_map/cond/branch_20_fun/ppermute | solution.py:412
  8.4 1.3 %collective-permute-start.61 = (bf16[128,1024]{1,0:T(8,128)(2,1)S(1)}, bf16[128,1024]{1,0:T(8,128)(2,1)}, u32[]{:S(2)}, u32[]{:S(2)}) collective-permute-start(bf16[128,1024]{1,0:T(8,128)(2,1)S(1)} %get-tuple-element.340), channel_id=1, source_target_pairs={{0,8},{4,12},{1,9},{5,13},{2,10},{6,14},{3,11},{7,15},{16,24},{20,... | collective-permute-start | bytes 786440 | tf_op jit(solution)/shard_map/cond/branch_20_fun/ppermute | solution.py:412
  9.7 0.1 collective-permute-start.56
  9.8 0.0 collective-permute-done.57
  9.8 0.5 %collective-permute-start.58 = (bf16[128,1024]{1,0:T(8,128)(2,1)}, bf16[128,1024]{1,0:T(8,128)(2,1)}, u32[]{:S(2)}, u32[]{:S(2)}) collective-permute-start(bf16[128,1024]{1,0:T(8,128)(2,1)} %collective-permute-done.57), channel_id=1, source_target_pairs={{1,0},{0,1},{3,2},{2,3},{5,4},{4,5},{7,6},{6,7},{9,8},{8,9},{11,10... | collective-permute-start | bytes 786440 | tf_op jit(solution)/shard_map/cond/branch_20_fun/ppermute | solution.py:407
  10.3 8.9 %collective-permute-done.59 = bf16[128,1024]{1,0:T(8,128)(2,1)} collective-permute-done((bf16[128,1024]{1,0:T(8,128)(2,1)S(1)}, bf16[128,1024]{1,0:T(8,128)(2,1)}, u32[]{:S(2)}, u32[]{:S(2)}) %collective-permute-start.59) | collective-permute-done | bytes 262176 | tf_op jit(solution)/shard_map/cond/branch_20_fun/ppermute | solution.py:412
  19.1 0.0 collective-permute-start.60
  19.1 12.4 %collective-permute-done.61 = bf16[128,1024]{1,0:T(8,128)(2,1)} collective-permute-done((bf16[128,1024]{1,0:T(8,128)(2,1)S(1)}, bf16[128,1024]{1,0:T(8,128)(2,1)}, u32[]{:S(2)}, u32[]{:S(2)}) %collective-permute-start.61) | collective-permute-done | bytes 262176 | tf_op jit(solution)/shard_map/cond/branch_20_fun/ppermute | solution.py:412
  31.5 0.0 collective-permute-start.62
  31.5 0.0 collective-permute-done.56
  31.5 0.0 collective-permute-done.58
  31.5 1.9 %collective-permute-done.62 = bf16[128,1024]{1,0:T(8,128)(2,1)} collective-permute-done((bf16[128,1024]{1,0:T(8,128)(2,1)}, bf16[128,1024]{1,0:T(8,128)(2,1)}, u32[]{:S(2)}, u32[]{:S(2)}) %collective-permute-start.62) | collective-permute-done | bytes 262176 | tf_op jit(solution)/shard_map/cond/branch_20_fun/ppermute | solution.py:407
  33.4 3.0 %lags_to_send.1 = bf16[4,3,128,128]{3,2,1,0:T(8,128)(2,1)S(1)} custom-call(s32[2,4]{1,0:T(2,128)S(1)} %bitcast.3, s32[4]{0:T(128)S(1)} %copy-done.1, f32[2,8,512]{2,1,0:T(8,128)S(1)} %copy-done.3, bf16[2,16,512]{2,1,0:T(8,128)(2,1)S(1)} %copy-done.2, bf16[128,1024]{1,0:T(8,128)(2,1)S(1)} %get-tuple-element.395.refs_4_, ...), custom_call_target="tpu_custom_call" | custom-call | flops 805306368 | bytes 3145728 | tf_op jit(solution)/shard_map/lags_to_send/pallas_call | solution.py:451
  36.4 1.6 %collective-permute-start.228 = (bf16[4,3,128,128]{3,2,1,0:T(8,128)(2,1)S(1)}, bf16[4,3,128,128]{3,2,1,0:T(8,128)(2,1)S(1)}, u32[]{:S(2)}, u32[]{:S(2)}) collective-permute-start(bf16[4,3,128,128]{3,2,1,0:T(8,128)(2,1)S(1)} %lags_to_send.1), channel_id=1, source_target_pairs={{0,2},{2,0},{1,3},{3,1},{4,6},{6,4},{5,7},{7,5},{8,10},{10,8},{9,1... | collective-permute-start | bytes 1179656 | tf_op jit(solution)/shard_map/ppermute | solution.py:477
  37.9 2.7 %lags_to_keep.1 = f32[4,3,128,128]{3,2,1,0:T(8,128)S(1)} custom-call(s32[2,4]{1,0:T(2,128)S(1)} %bitcast.4, s32[4]{0:T(128)S(1)} %copy-done.1, f32[2,8,512]{2,1,0:T(8,128)S(1)} %copy-done.3, bf16[2,16,512]{2,1,0:T(8,128)(2,1)S(1)} %copy-done.2, bf16[128,1024]{1,0:T(8,128)(2,1)S(1)} %get-tuple-element.395.refs_4_, ...), custom_call_target="tpu_custom_call" | custom-call | flops 805306368 | bytes 3145728 | tf_op jit(solution)/shard_map/lags_to_keep/pallas_call | solution.py:451
  40.7 6.9 %collective-permute-done.228 = bf16[4,3,128,128]{3,2,1,0:T(8,128)(2,1)S(1)} collective-permute-done((bf16[4,3,128,128]{3,2,1,0:T(8,128)(2,1)S(1)}, bf16[4,3,128,128]{3,2,1,0:T(8,128)(2,1)S(1)}, u32[]{:S(2)}, u32[]{:S(2)}) %collective-permute-start.228) | collective-permute-done | bytes 393248 | tf_op jit(solution)/shard_map/ppermute | solution.py:477
  47.6 0.9 %multiply_convert_fusion = bf16[4,3,128,128]{3,2,1,0:T(8,128)(2,1)} fusion(f32[4,3,128,128]{3,2,1,0:T(8,128)S(1)} %lags_to_keep.1, bf16[4,3,128,128]{3,2,1,0:T(8,128)(2,1)S(1)} %collective-permute-done.228), kind=kLoop, calls=%fused_computation.18 | loop fusion | flops 786432 | bytes 1572864 | tf_op jit(solution)/shard_map/convert_element_type | solution.py:481
  (5 shorter events, 0.0 us)
Async XLA Ops:
  4.5 28.9 %copy-start = (s32[4,2]{0,1:T(2,128)S(1)}, s32[4,2]{0,1:T(2,128)}, u32[]{:S(2)}) copy-start(s32[4,2]{0,1:T(2,128)} %param.38) | copy-start | bytes 100
  4.5 28.9 %copy-start.1 = (s32[4]{0:T(128)S(1)}, s32[4]{0:T(128)}, u32[]{:S(2)}) copy-start(s32[4]{0:T(128)} %refs_1_.3) | copy-start | bytes 52
  4.5 28.9 %copy-start.2 = (bf16[2,16,512]{2,1,0:T(8,128)(2,1)S(1)}, bf16[2,16,512]{2,1,0:T(8,128)(2,1)}, u32[]{:S(2)}) copy-start(bf16[2,16,512]{2,1,0:T(8,128)(2,1)} %constant.142.clone.refs_3_) | copy-start | bytes 98308
  4.5 28.9 %copy-start.3 = (f32[2,8,512]{2,1,0:T(8,128)S(1)}, f32[2,8,512]{2,1,0:T(8,128)}, u32[]{:S(2)}) copy-start(f32[2,8,512]{2,1,0:T(8,128)} %constant.141.clone.refs_2_) | copy-start | bytes 98308
  4.7 5.0 %collective-permute-start.57 = (bf16[128,1024]{1,0:T(8,128)(2,1)S(1)}, bf16[128,1024]{1,0:T(8,128)(2,1)}, u32[]{:S(2)}, u32[]{:S(2)}) collective-permute-start(bf16[128,1024]{1,0:T(8,128)(2,1)S(1)} %get-tuple-element.338), channel_id=1, source_target_pairs={{4,8},{5,9},{6,10},{7,11},{20,24},{21,25},{22,26},{23,27}} | collective-permute-start | bytes 786440 | tf_op jit(solution)/shard_map/cond/branch_20_fun/ppermute | solution.py:412
  6.1 13.0 %collective-permute-start.59 = (bf16[128,1024]{1,0:T(8,128)(2,1)S(1)}, bf16[128,1024]{1,0:T(8,128)(2,1)}, u32[]{:S(2)}, u32[]{:S(2)}) collective-permute-start(bf16[128,1024]{1,0:T(8,128)(2,1)S(1)} %get-tuple-element.339), channel_id=1, source_target_pairs={{12,8},{0,12},{13,9},{1,13},{14,10},{2,14},{15,11},{3,15},{28,24},... | collective-permute-start | bytes 786440 | tf_op jit(solution)/shard_map/cond/branch_20_fun/ppermute | solution.py:412
  8.4 23.1 %collective-permute-start.61 = (bf16[128,1024]{1,0:T(8,128)(2,1)S(1)}, bf16[128,1024]{1,0:T(8,128)(2,1)}, u32[]{:S(2)}, u32[]{:S(2)}) collective-permute-start(bf16[128,1024]{1,0:T(8,128)(2,1)S(1)} %get-tuple-element.340), channel_id=1, source_target_pairs={{0,8},{4,12},{1,9},{5,13},{2,10},{6,14},{3,11},{7,15},{16,24},{20,... | collective-permute-start | bytes 786440 | tf_op jit(solution)/shard_map/cond/branch_20_fun/ppermute | solution.py:412
  9.7 21.8 %collective-permute-start.56 = (bf16[128,1024]{1,0:T(8,128)(2,1)S(1)}, bf16[128,1024]{1,0:T(8,128)(2,1)}, u32[]{:S(2)}, u32[]{:S(2)}) collective-permute-start(bf16[128,1024]{1,0:T(8,128)(2,1)S(1)} %get-tuple-element.337), channel_id=1, source_target_pairs={{1,0},{0,1},{3,2},{2,3},{5,4},{4,5},{7,6},{6,7},{9,8},{8,9},{11,10... | collective-permute-start | bytes 786440 | tf_op jit(solution)/shard_map/cond/branch_20_fun/ppermute | solution.py:407
  9.8 21.7 %collective-permute-start.58 = (bf16[128,1024]{1,0:T(8,128)(2,1)}, bf16[128,1024]{1,0:T(8,128)(2,1)}, u32[]{:S(2)}, u32[]{:S(2)}) collective-permute-start(bf16[128,1024]{1,0:T(8,128)(2,1)} %collective-permute-done.57), channel_id=1, source_target_pairs={{1,0},{0,1},{3,2},{2,3},{5,4},{4,5},{7,6},{6,7},{9,8},{8,9},{11,10... | collective-permute-start | bytes 786440 | tf_op jit(solution)/shard_map/cond/branch_20_fun/ppermute | solution.py:407
  19.1 12.4 %collective-permute-start.60 = (bf16[128,1024]{1,0:T(8,128)(2,1)}, bf16[128,1024]{1,0:T(8,128)(2,1)}, u32[]{:S(2)}, u32[]{:S(2)}) collective-permute-start(bf16[128,1024]{1,0:T(8,128)(2,1)} %collective-permute-done.59), channel_id=1, source_target_pairs={{1,0},{0,1},{3,2},{2,3},{5,4},{4,5},{7,6},{6,7},{9,8},{8,9},{11,10... | collective-permute-start | bytes 786440 | tf_op jit(solution)/shard_map/cond/branch_20_fun/ppermute | solution.py:407
  31.5 1.9 %collective-permute-start.62 = (bf16[128,1024]{1,0:T(8,128)(2,1)}, bf16[128,1024]{1,0:T(8,128)(2,1)}, u32[]{:S(2)}, u32[]{:S(2)}) collective-permute-start(bf16[128,1024]{1,0:T(8,128)(2,1)} %collective-permute-done.61), channel_id=1, source_target_pairs={{1,0},{0,1},{3,2},{2,3},{5,4},{4,5},{7,6},{6,7},{9,8},{8,9},{11,10... | collective-permute-start | bytes 786440 | tf_op jit(solution)/shard_map/cond/branch_20_fun/ppermute | solution.py:407
  36.4 11.2 %collective-permute-start.228 = (bf16[4,3,128,128]{3,2,1,0:T(8,128)(2,1)S(1)}, bf16[4,3,128,128]{3,2,1,0:T(8,128)(2,1)S(1)}, u32[]{:S(2)}, u32[]{:S(2)}) collective-permute-start(bf16[4,3,128,128]{3,2,1,0:T(8,128)(2,1)S(1)} %lags_to_send.1), channel_id=1, source_target_pairs={{0,2},{2,0},{1,3},{3,1},{4,6},{6,4},{5,7},{7,5},{8,10},{10,8},{9,1... | collective-permute-start | bytes 1179656 | tf_op jit(solution)/shard_map/ppermute | solution.py:477

commit v2 on v1

--- a/solution.py
+++ b/solution.py
@@ -33,13 +33,34 @@
     return lax.broadcasted_iota(jnp.int32, shape, dim)
 
 
-def send_keys(first, second, sta_count, where):
-    keys = []
-    for reach in range(1, REACH):
-        distance = abs((first + reach) % sta_count - first)
-        alone = (first - second - reach) % sta_count == 0
-        keys.append((2 * distance + where(alone, 0, 1)) * REACH + reach)
-    return keys
+def schedule(first, second, sta_count):
+    every = range(1, REACH)
+    if 0 < first < sta_count - 1:
+        ring = 1 if 2 * first < sta_count else REACH - 1
+        pairs = [((home + ring) % sta_count, home) for home in range(sta_count)]
+    else:
+        pairs = [(home ^ 1, home) for home in range(sta_count)]
+    source = {target: start for start, target in pairs}
+    reaches = [[(source[owner] - owner) % sta_count] for owner in (first, second)]
+    both = [reach for reach in every if [reach] not in reaches]
+    for taken in reaches:
+        taken += both + [reach for reach in every if reach not in taken + both]
+    plan = [(True, pairs, reaches[0][0], reaches[1][0])]
+    for one, other in zip(reaches[0][1:], reaches[1][1:]):
+        flows = [((first + one) % sta_count, first), ((second + other) % sta_count, second)]
+        plan.append((False, flows, one, other))
+    return plan[:1] + sorted(plan[1:], key=lambda step: step[1][1][0] == first)
+
+
+def place_table(sta_count):
+    table = []
+    for first, second in itertools.product(range(sta_count), repeat=2):
+        places = [0] * (2 * REACH)
+        if first != second:
+            for place, step in enumerate(schedule(first, second, sta_count)):
+                places[step[2]], places[REACH + step[3]] = place + 1, place + 1
+        table += places
+    return table
 
 
 def read_pairs(pair_ref, owner_ref, block_count):
@@ -134,8 +155,15 @@
     hot = jnp.where(station == iota((tiles * LANES, kept * width), 0), 1.0, 0.0).astype(BF16)
 
     if branched:
-        number_ref[0] = case_ref[case_of(pairs, sta_count)[2]]
+        first, second, case = case_of(pairs, sta_count)
+        number_ref[0] = case_ref[case]
         branch_copy.start()
+        base = case_number(sta_count, 0, 0, sta_count) + (first * sta_count + second) * 2 * REACH
+        for place, reach_here in enumerate(places):
+            reach = jnp.maximum(reach_here, 0)
+            owner = lax.rem(my_sta - reach + REACH * sta_count, sta_count)
+            step = case_ref[base + jnp.where(owner == first, 0, REACH) + reach]
+            places[place] = jnp.where(reach_here < 0, -1, step)
 
     for part in range(COPIES):
         fetch(part).wait()
@@ -227,23 +255,24 @@
 def routes(sta_count):
     def load(first, second, sent):
         links = {}
-        flows = [((first + reach) % sta_count, first) for reach in range(1, REACH)]
-        flows += [((second + reach) % sta_count, second) for reach in sent]
-        for source, owner in flows:
-            step = 1 if owner > source else -1
-            for place in range(source, owner, step):
-                links[place, step] = links.get((place, step), 0) + 1
+        for full, flows, _, other in schedule(first, second, sta_count):
+            for source, owner in flows if full or other in sent else flows[:1]:
+                step = 1 if owner > source else -1
+                for place in range(source, owner, step):
+                    links[place, step] = links.get((place, step), 0) + 1
         return max(links.values())
 
-    every = range(1, REACH)
-    sets = [every, *itertools.combinations(every, len(every) - 1)]
     branches = []
     cases = [0] * case_number(sta_count, 0, 0, sta_count)
     for first, second in itertools.permutations(range(sta_count), 2):
-        own = (first - second) % sta_count
+        others = [step[3] for step in schedule(first, second, sta_count) if not step[0]]
+        sets = [
+            sent
+            for count in range(len(others), -1, -1)
+            for sent in itertools.combinations(others, count)
+        ]
         for named in itertools.combinations(range(REACH), 2):
-            fits = [sent for sent in sets if set(named) - {0} <= set(sent)]
-            fits = [sent for sent in fits if own in named or own not in sent] or fits
+            fits = [sent for sent in sets if set(named) & set(others) <= set(sent)]
             branch = (first, second, min(fits, key=lambda sent: load(first, second, sent)))
             if branch not in branches:
                 branches.append(branch)
@@ -275,8 +304,8 @@
 def lag_kernel(hops, slots, lag_rows, away, block_count, branched, *refs):
     sub_count = lax.axis_size("sub")
     hr_count = lax.axis_size("hr")
-    pair_ref, owner_ref, turn_ref, offset_ref = refs[:4]
-    blocks, outs = refs[4 : -2 - len(hops)], refs[-2 - len(hops) : -2]
+    pair_ref, owner_ref, place_ref, turn_ref, offset_ref = refs[:5]
+    blocks, outs = refs[5 : -2 - len(hops)], refs[-2 - len(hops) : -2]
     buf, sems = refs[-2:]
     width = buf.shape[3]
     span = buf.shape[4] // 2
@@ -290,9 +319,8 @@
     order = [jnp.int32(reach) for reach in range(REACH)]
     if branched:
         first, second, _ = case_of(pairs, sta_count)
-        keys = send_keys(first, second, sta_count, jnp.where)
-        for reach, key in enumerate(keys):
-            order[1 + reach] = 1 + sum(jnp.int32(other < key) for other in keys)
+        entry = (first * sta_count + second) * 2 + (my_sta != first).astype(jnp.int32)
+        order = [place_ref[entry * REACH + reach] for reach in range(REACH)]
     owned = []
     for owner, _, homes in pairs:
         places = []
@@ -394,8 +422,10 @@
     owners_at_most = pair_owner.shape[0] - CAP + 1
     branched = owners_at_most == 2 and sta_count == REACH
     kept = min(REACH, owners_at_most)
-    branches, cases = routes(sta_count) if branched else ([], [])
-    case_table = jnp.asarray(np.array(cases or [0], dtype=np.int32))
+    branches, cases = routes(sta_count) if branched else ([], [0])
+    places = place_table(sta_count) if branched else [0]
+    case_table = jnp.asarray(np.array(cases + places, dtype=np.int32))
+    places = jnp.asarray(np.array(places, dtype=np.int32))
     picked = pick_blocks(
         kept, branched, spectra, pair_sides, pair_owner, block_members, case_table
     )
@@ -407,32 +437,18 @@
             blocks.append(lax.ppermute(block, "sub", swap))
         return blocks
 
-    def to_owners(block, reach, owners):
-        pairs = [((owner + reach) % sta_count, owner) for owner in owners]
-        return lax.ppermute(block, "sta", pairs)
-
     def exchange(*picked):
-        blocks = []
+        blocks = halves(picked[0])
         for reach in range(1, REACH):
-            blocks += halves(to_owners(picked[reach], reach, range(sta_count)))
-        return halves(picked[0]) + blocks
+            shift = [((home + reach) % sta_count, home) for home in range(sta_count)]
+            blocks += halves(lax.ppermute(picked[reach], "sta", shift))
+        return blocks
 
     def exchange_two(first, second, sent, *picked):
-        own = (first - second) % sta_count
-        keys = send_keys(first, second, sta_count, lambda hit, yes, no: yes if hit else no)
-        order = sorted(range(1, REACH), key=lambda reach: keys[reach - 1])
-        arrived = {}
-        for reach in order:
-            owners = (first, second) if reach in sent and reach != own else (first,)
-            arrived[reach] = to_owners(picked[reach], reach, owners)
-        if own in sent:
-            block, _ = lax.optimization_barrier((picked[own], arrived[order[0]]))
-            block = to_owners(block, own, (second,))
-            here = lax.axis_index("sta") == second
-            arrived[own] = jnp.where(here, block, arrived[own])
         blocks = halves(picked[0])
-        for reach in order:
-            blocks += halves(arrived[reach])
+        for block, (full, flows, _, other) in zip(picked[1:], schedule(first, second, sta_count)):
+            flows = flows if full or other in sent else flows[:1]
+            blocks += halves(lax.ppermute(block, "sta", flows))
         return blocks
 
     if branched:
@@ -454,7 +470,7 @@
             ),
             out_shape=[jax.ShapeDtypeStruct((lag_rows, len(slots), width, width), dtype)]
             * len(hops),
-            in_specs=[smem, smem, vmem, vmem] + [hbm] * len(blocks),
+            in_specs=[smem, smem, smem, vmem, vmem] + [hbm] * len(blocks),
             out_specs=[vmem] * len(hops),
             scratch_shapes=[
                 pltpu.VMEM((len(slots), 2, sub_count, width, row), BF16),
@@ -467,7 +483,7 @@
                 transcendentals=0,
             ),
             name=name,
-        )(pair_sides, pair_owner, turns, offsets, *blocks)
+        )(pair_sides, pair_owner, places, turns, offsets, *blocks)
 
     hops, slots = tuple(range(1, hr_count)), tuple(range(CAP))
     sent = products(hops, slots, BF16, "lags_to_send")

time: 47.6 us -> 43.4 us (0.912)
  the two profiles are of different devices: /device:TPU:24 before, /device:TPU:0 now
where the time goes in v2:
time: 43.4 us; the launch traced here: 43 us
  waiting for transfers between devices  20.7 us (48%)
  starting transfers between devices  11.1 us (26%)
  Pallas kernels  9.29 us (21%)
  other arithmetic  0.86 us (2%)
  between operations  0.7 us (2%)
    ppermute x3, waiting for transfers between devices, exchange_two(): blocks += halves(lax.ppermute(block, 'sta', flows))  11.9 us
    ppermute x3, starting transfers between devices, exchange_two(): blocks += halves(lax.ppermute(block, 'sta', flows))  8.75 us
    ppermute x1, waiting for transfers between devices, on_device(): received.append(lax.ppermute(part, 'hr', to_device))  6.79 us
    pallas_call x2, Pallas kernels, products(): pl.pallas_call(functools.partial(lag_kernel, hops, slots, lag_rows, away,...  5.43 us
    pallas_call x1, Pallas kernels, pick_blocks(): pl.pallas_call(functools.partial(pick_kernel, kept, branched, 'sta'), out...  3.86 us
    ppermute x4, waiting for transfers between devices, halves(): blocks.append(lax.ppermute(block, 'sub', swap))  2.04 us
    ppermute x1, starting transfers between devices, on_device(): received.append(lax.ppermute(part, 'hr', to_device))  1.72 us
  transfers between devices with their start and end apart: 8, of which 5 were waited for; matrix products, arithmetic and copies ran while one was open for 0% of the time, Pallas kernels for 6%

profile of v2, /device:TPU:0, one launch (start us, length us, event | category | flops | bytes accessed | tf_op | source)
XLA Modules:
  0.0 43.0 jit_solution(18387843459366612306)
XLA Ops:
  0.0 3.9 %pick_and_whiten.1 = (bf16[128,1024]{1,0:T(8,128)(2,1)S(1)}, bf16[128,1024]{1,0:T(8,128)(2,1)S(1)}, bf16[128,1024]{1,0:T(8,128)(2,1)S(1)}, bf16[128,1024]{1,0:T(8,128)(2,1)S(1)}, s32[1]{0:T(128)}) custom-call(s32[2,4]{1,0:T(2,128)} %bitcast.2, s32[4]{0:T(128)} %refs_1_.3, s32[8,128]{1,0:T(8,128)} %member_hbm.1, s32[256]{0:T(256)} %constant.16.clone.case_hbm, ...), custom_call_target="tpu_custom_call" | custom-call | flops 524288000 | bytes 3096576 | tf_op jit(solution)/shard_map/pick_and_whiten/pallas_call | solution.py:225
  4.5 23.6 %conditional.1 = (bf16[128,1024]{1,0:T(8,128)(2,1)}, bf16[128,1024]{1,0:T(8,128)(2,1)}, bf16[128,1024]{1,0:T(8,128)(2,1)}, bf16[128,1024]{1,0:T(8,128)(2,1)}, bf...) conditional(s32[]{:T(128)} %bitcast.1, ...), branch_computations={%region_0.0_spmd, %region_1.0_spmd, %region_2.0_spmd, %region_3.0_... | conditional | bytes 7340368 | solution.py:456
  4.8 3.1 %collective-permute-start.162 = (bf16[128,1024]{1,0:T(8,128)(2,1)S(1)}, bf16[128,1024]{1,0:T(8,128)(2,1)}, u32[]{:S(2)}, u32[]{:S(2)}) collective-permute-start(bf16[128,1024]{1,0:T(8,128)(2,1)S(1)} %get-tuple-element.322), channel_id=1, source_target_pairs={{4,0},{0,4},{12,8},{8,12},{5,1},{1,5},{13,9},{9,13},{6,2},{2,6},{1... | collective-permute-start | bytes 786440 | tf_op jit(solution)/shard_map/cond/branch_23_fun/ppermute | solution.py:451
  7.8 1.3 %collective-permute-start.164 = (bf16[128,1024]{1,0:T(8,128)(2,1)S(1)}, bf16[128,1024]{1,0:T(8,128)(2,1)}, u32[]{:S(2)}, u32[]{:S(2)}) collective-permute-start(bf16[128,1024]{1,0:T(8,128)(2,1)S(1)} %get-tuple-element.323), channel_id=1, source_target_pairs={{4,12},{8,0},{5,13},{9,1},{6,14},{10,2},{7,15},{11,3},{20,28},{24,... | collective-permute-start | bytes 786440 | tf_op jit(solution)/shard_map/cond/branch_23_fun/ppermute | solution.py:451
  9.1 4.4 %collective-permute-start.166 = (bf16[128,1024]{1,0:T(8,128)(2,1)S(1)}, bf16[128,1024]{1,0:T(8,128)(2,1)}, u32[]{:S(2)}, u32[]{:S(2)}) collective-permute-start(bf16[128,1024]{1,0:T(8,128)(2,1)S(1)} %get-tuple-element.324), channel_id=1, source_target_pairs={{0,12},{12,0},{1,13},{13,1},{2,14},{14,2},{3,15},{15,3},{16,28},{2... | collective-permute-start | bytes 786440 | tf_op jit(solution)/shard_map/cond/branch_23_fun/ppermute | solution.py:451
  13.5 0.1 collective-permute-start.161
  13.6 11.9 %collective-permute-done.162 = bf16[128,1024]{1,0:T(8,128)(2,1)} collective-permute-done((bf16[128,1024]{1,0:T(8,128)(2,1)S(1)}, bf16[128,1024]{1,0:T(8,128)(2,1)}, u32[]{:S(2)}, u32[]{:S(2)}) %collective-permute-start.162) | collective-permute-done | bytes 262176 | tf_op jit(solution)/shard_map/cond/branch_23_fun/ppermute | solution.py:451
  25.5 0.0 collective-permute-start.163
  25.5 0.0 collective-permute-done.164
  25.5 0.5 %collective-permute-start.165 = (bf16[128,1024]{1,0:T(8,128)(2,1)}, bf16[128,1024]{1,0:T(8,128)(2,1)}, u32[]{:S(2)}, u32[]{:S(2)}) collective-permute-start(bf16[128,1024]{1,0:T(8,128)(2,1)} %collective-permute-done.164), channel_id=1, source_target_pairs={{1,0},{0,1},{3,2},{2,3},{5,4},{4,5},{7,6},{6,7},{9,8},{8,9},{11,10... | collective-permute-start | bytes 786440 | tf_op jit(solution)/shard_map/cond/branch_23_fun/ppermute | solution.py:437
  26.0 0.0 collective-permute-done.166
  26.0 0.1 collective-permute-start.167
  26.1 0.0 collective-permute-done.161
  26.1 1.3 %collective-permute-done.163 = bf16[128,1024]{1,0:T(8,128)(2,1)} collective-permute-done((bf16[128,1024]{1,0:T(8,128)(2,1)}, bf16[128,1024]{1,0:T(8,128)(2,1)}, u32[]{:S(2)}, u32[]{:S(2)}) %collective-permute-start.163) | collective-permute-done | bytes 262176 | tf_op jit(solution)/shard_map/cond/branch_23_fun/ppermute | solution.py:437
  27.4 0.4 collective-permute-done.165
  27.7 0.4 collective-permute-done.167
  28.1 0.0 copy-done.2
  28.1 0.0 copy-done.3
  28.1 0.0 copy-done.4
  28.1 2.7 %lags_to_send.1 = bf16[4,3,128,128]{3,2,1,0:T(8,128)(2,1)S(1)} custom-call(s32[2,4]{1,0:T(2,128)S(1)} %bitcast.3, s32[4]{0:T(128)S(1)} %copy-done.1, s32[128]{0:T(128)S(1)} %copy-done.4, f32[2,8,512]{2,1,0:T(8,128)S(1)} %copy-done.3, bf16[2,16,512]{2,1,0:T(8,128)(2,1)S(1)} %copy-done.2, bf16[128,1024]{1,0:T(8,128)(2,1)S(1)} %get-tuple-element.353.refs_5_, ...), custom_call_target="tpu_custom_call" | custom-call | flops 805306368 | bytes 3145728 | tf_op jit(solution)/shard_map/lags_to_send/pallas_call | solution.py:467
  30.9 1.7 %collective-permute-start.196 = (bf16[4,3,128,128]{3,2,1,0:T(8,128)(2,1)S(1)}, bf16[4,3,128,128]{3,2,1,0:T(8,128)(2,1)S(1)}, u32[]{:S(2)}, u32[]{:S(2)}) collective-permute-start(bf16[4,3,128,128]{3,2,1,0:T(8,128)(2,1)S(1)} %lags_to_send.1), channel_id=1, source_target_pairs={{0,2},{2,0},{1,3},{3,1},{4,6},{6,4},{5,7},{7,5},{8,10},{10,8},{9,1... | collective-permute-start | bytes 1179656 | tf_op jit(solution)/shard_map/ppermute | solution.py:493
  32.6 2.7 %lags_to_keep.1 = f32[4,3,128,128]{3,2,1,0:T(8,128)S(1)} custom-call(s32[2,4]{1,0:T(2,128)S(1)} %bitcast.4, s32[4]{0:T(128)S(1)} %copy-done.1, s32[128]{0:T(128)S(1)} %copy-done.4, f32[2,8,512]{2,1,0:T(8,128)S(1)} %copy-done.3, bf16[2,16,512]{2,1,0:T(8,128)(2,1)S(1)} %copy-done.2, bf16[128,1024]{1,0:T(8,128)(2,1)S(1)} %get-tuple-element.353.refs_5_, ...), custom_call_target="tpu_custom_call" | custom-call | flops 805306368 | bytes 3145728 | tf_op jit(solution)/shard_map/lags_to_keep/pallas_call | solution.py:467
  35.3 6.8 %collective-permute-done.196 = bf16[4,3,128,128]{3,2,1,0:T(8,128)(2,1)S(1)} collective-permute-done((bf16[4,3,128,128]{3,2,1,0:T(8,128)(2,1)S(1)}, bf16[4,3,128,128]{3,2,1,0:T(8,128)(2,1)S(1)}, u32[]{:S(2)}, u32[]{:S(2)}) %collective-permute-start.196) | collective-permute-done | bytes 393248 | tf_op jit(solution)/shard_map/ppermute | solution.py:493
  42.1 0.9 %multiply_convert_fusion = bf16[4,3,128,128]{3,2,1,0:T(8,128)(2,1)} fusion(f32[4,3,128,128]{3,2,1,0:T(8,128)S(1)} %lags_to_keep.1, bf16[4,3,128,128]{3,2,1,0:T(8,128)(2,1)S(1)} %collective-permute-done.196), kind=kLoop, calls=%fused_computation | loop fusion | flops 786432 | bytes 1572864 | tf_op jit(solution)/shard_map/convert_element_type | solution.py:497
  (7 shorter events, 0.0 us)
Async XLA Ops:
  0.0 28.1 %copy-start.2 = (bf16[2,16,512]{2,1,0:T(8,128)(2,1)S(1)}, bf16[2,16,512]{2,1,0:T(8,128)(2,1)}, u32[]{:S(2)}) copy-start(bf16[2,16,512]{2,1,0:T(8,128)(2,1)} %constant.19.clone.refs_4_) | copy-start | bytes 98308
  0.0 28.1 %copy-start.3 = (f32[2,8,512]{2,1,0:T(8,128)S(1)}, f32[2,8,512]{2,1,0:T(8,128)}, u32[]{:S(2)}) copy-start(f32[2,8,512]{2,1,0:T(8,128)} %constant.18.clone.refs_3_) | copy-start | bytes 98308
  0.0 28.1 %copy-start.4 = (s32[128]{0:T(128)S(1)}, s32[128]{0:T(128)}, u32[]{:S(2)}) copy-start(s32[128]{0:T(128)} %constant.17.clone.refs_2_) | copy-start | bytes 1540
  0.0 28.1 %copy-start.1 = (s32[4]{0:T(128)S(1)}, s32[4]{0:T(128)}, u32[]{:S(2)}) copy-start(s32[4]{0:T(128)} %refs_1_.3) | copy-start | bytes 52
  0.0 28.1 %copy-start = (s32[4,2]{0,1:T(2,128)S(1)}, s32[4,2]{0,1:T(2,128)}, u32[]{:S(2)}) copy-start(s32[4,2]{0,1:T(2,128)} %param.37) | copy-start | bytes 100
  4.8 20.7 %collective-permute-start.162 = (bf16[128,1024]{1,0:T(8,128)(2,1)S(1)}, bf16[128,1024]{1,0:T(8,128)(2,1)}, u32[]{:S(2)}, u32[]{:S(2)}) collective-permute-start(bf16[128,1024]{1,0:T(8,128)(2,1)S(1)} %get-tuple-element.322), channel_id=1, source_target_pairs={{4,0},{0,4},{12,8},{8,12},{5,1},{1,5},{13,9},{9,13},{6,2},{2,6},{1... | collective-permute-start | bytes 786440 | tf_op jit(solution)/shard_map/cond/branch_23_fun/ppermute | solution.py:451
  7.8 17.7 %collective-permute-start.164 = (bf16[128,1024]{1,0:T(8,128)(2,1)S(1)}, bf16[128,1024]{1,0:T(8,128)(2,1)}, u32[]{:S(2)}, u32[]{:S(2)}) collective-permute-start(bf16[128,1024]{1,0:T(8,128)(2,1)S(1)} %get-tuple-element.323), channel_id=1, source_target_pairs={{4,12},{8,0},{5,13},{9,1},{6,14},{10,2},{7,15},{11,3},{20,28},{24,... | collective-permute-start | bytes 786440 | tf_op jit(solution)/shard_map/cond/branch_23_fun/ppermute | solution.py:451
  9.1 16.9 %collective-permute-start.166 = (bf16[128,1024]{1,0:T(8,128)(2,1)S(1)}, bf16[128,1024]{1,0:T(8,128)(2,1)}, u32[]{:S(2)}, u32[]{:S(2)}) collective-permute-start(bf16[128,1024]{1,0:T(8,128)(2,1)S(1)} %get-tuple-element.324), channel_id=1, source_target_pairs={{0,12},{12,0},{1,13},{13,1},{2,14},{14,2},{3,15},{15,3},{16,28},{2... | collective-permute-start | bytes 786440 | tf_op jit(solution)/shard_map/cond/branch_23_fun/ppermute | solution.py:451
  13.5 12.6 %collective-permute-start.161 = (bf16[128,1024]{1,0:T(8,128)(2,1)S(1)}, bf16[128,1024]{1,0:T(8,128)(2,1)}, u32[]{:S(2)}, u32[]{:S(2)}) collective-permute-start(bf16[128,1024]{1,0:T(8,128)(2,1)S(1)} %get-tuple-element.321), channel_id=1, source_target_pairs={{1,0},{0,1},{3,2},{2,3},{5,4},{4,5},{7,6},{6,7},{9,8},{8,9},{11,10... | collective-permute-start | bytes 786440 | tf_op jit(solution)/shard_map/cond/branch_23_fun/ppermute | solution.py:437
  25.5 1.9 %collective-permute-start.163 = (bf16[128,1024]{1,0:T(8,128)(2,1)}, bf16[128,1024]{1,0:T(8,128)(2,1)}, u32[]{:S(2)}, u32[]{:S(2)}) collective-permute-start(bf16[128,1024]{1,0:T(8,128)(2,1)} %collective-permute-done.162), channel_id=1, source_target_pairs={{1,0},{0,1},{3,2},{2,3},{5,4},{4,5},{7,6},{6,7},{9,8},{8,9},{11,10... | collective-permute-start | bytes 786440 | tf_op jit(solution)/shard_map/cond/branch_23_fun/ppermute | solution.py:437
  25.5 2.2 %collective-permute-start.165 = (bf16[128,1024]{1,0:T(8,128)(2,1)}, bf16[128,1024]{1,0:T(8,128)(2,1)}, u32[]{:S(2)}, u32[]{:S(2)}) collective-permute-start(bf16[128,1024]{1,0:T(8,128)(2,1)} %collective-permute-done.164), channel_id=1, source_target_pairs={{1,0},{0,1},{3,2},{2,3},{5,4},{4,5},{7,6},{6,7},{9,8},{8,9},{11,10... | collective-permute-start | bytes 786440 | tf_op jit(solution)/shard_map/cond/branch_23_fun/ppermute | solution.py:437
  26.0 2.1 %collective-permute-start.167 = (bf16[128,1024]{1,0:T(8,128)(2,1)}, bf16[128,1024]{1,0:T(8,128)(2,1)}, u32[]{:S(2)}, u32[]{:S(2)}) collective-permute-start(bf16[128,1024]{1,0:T(8,128)(2,1)} %collective-permute-done.166), channel_id=1, source_target_pairs={{1,0},{0,1},{3,2},{2,3},{5,4},{4,5},{7,6},{6,7},{9,8},{8,9},{11,10... | collective-permute-start | bytes 786440 | tf_op jit(solution)/shard_map/cond/branch_23_fun/ppermute | solution.py:437
  30.9 11.2 %collective-permute-start.196 = (bf16[4,3,128,128]{3,2,1,0:T(8,128)(2,1)S(1)}, bf16[4,3,128,128]{3,2,1,0:T(8,128)(2,1)S(1)}, u32[]{:S(2)}, u32[]{:S(2)}) collective-permute-start(bf16[4,3,128,128]{3,2,1,0:T(8,128)(2,1)S(1)} %lags_to_send.1), channel_id=1, source_target_pairs={{0,2},{2,0},{1,3},{3,1},{4,6},{6,4},{5,7},{7,5},{8,10},{10,8},{9,1... | collective-permute-start | bytes 1179656 | tf_op jit(solution)/shard_map/ppermute | solution.py:493
